TPU v7x, 512 devices: a whole 4x8x8 slice. The times are simulated.
512 devices in a mesh: label: 64 (over y, x, core), query: 8 (over z).
Axes of the slice: x: 4, y: 8, z: 8, core: 2. Of those that a mesh axis runs over, the one named last changes fastest.
Arguments:
- queries: bfloat16 [1536, 768], P('query'), may hold values from -6 to 6
- label_ids: int32 [1536, 10], P('query'), may hold values from 0 to 4095, as said below
- label_text: bfloat16 [4096, 32, 768], P('label'), may hold values from -16 to 16
- up_weight: bfloat16 [768, 3072], P(None, 'query'), may hold values from -0.21875 to 0.21875
- down_weight: bfloat16 [768, 3072], P(None, 'query'), may hold values from -0.109375 to 0.109375
- free_vectors: float32 [4096, 768], P('label'), may hold values from -4 to 4
- moments: float32 [4096, 768], P('label'), may hold values from -0.06 to 0.06
- seconds: float32 [4096, 768], P('label'), may hold values from 1e-05 to 0.001
Outputs:
- free_new: float32 [4096, 768], P('label')
- moments_new: float32 [4096, 768], P('label')
- seconds_new: float32 [4096, 768], P('label')
- query_grad: float32 [1536, 768], P('query')
- up_grad: float32 [768, 3072], P('label', 'query')
- down_grad: float32 [768, 3072], P('label', 'query')
Inputs may be any that keep to these rules, and one draw needn't show every extreme that they name: `label_ids`: the 10 ids of one query are distinct.
All inputs are finite; a program needn't handle non-finite values.
Results may differ from a plain program's by a relative error of at most 0.023.
Values sent between devices are 32-bit elements; how exact they have to be, the bound alone decides.
A program may use at most 64 MiB of HBM per device.

v0:
```python
import jax
import jax.numpy as jnp
from jax import lax
from jax.sharding import PartitionSpec as P

beta_one = 0.9
beta_two = 0.999
adam_eps = 1e-08
learn_rate = 0.05
first_fix = 1.0 - 0.9**10
second_fix = 1.0 - 0.999**10


def gelu_tanh(values):
    return jax.nn.gelu(values, approximate=True)


def body(queries, label_ids, label_text, up_weight, down_weight, free_vectors, moments, seconds):
    label_rows, text_len, model_width = label_text.shape
    unit_cols = up_weight.shape[1]
    temper = 1.0 / jnp.sqrt(jnp.float32(model_width))
    text_rows = label_text.reshape(label_rows * text_len, model_width)
    preact = jnp.dot(text_rows, up_weight, preferred_element_type=jnp.float32)
    hidden = gelu_tanh(preact).astype(jnp.bfloat16)
    pooled_hidden = jnp.mean(
        hidden.reshape(label_rows, text_len, unit_cols), axis=1, dtype=jnp.float32
    )
    pooled_text = jnp.mean(label_text, axis=1, dtype=jnp.float32)
    encoded_part = jnp.einsum(
        "lf,df->ld", pooled_hidden, down_weight.astype(jnp.float32), precision=lax.Precision.HIGHEST
    )
    encoded = lax.psum(encoded_part, "query")
    label_vec = pooled_text + encoded + free_vectors
    label_bf = label_vec.astype(jnp.bfloat16)
    first_label = lax.axis_index("label") * label_rows
    local_ids = label_ids - first_label
    owners = (
        local_ids[:, :, None] == jnp.arange(label_rows, dtype=jnp.int32)[None, None, :]
    ).astype(jnp.float32)
    similar = jnp.einsum("id,jd->ij", queries, label_bf, preferred_element_type=jnp.float32)
    partial_value = jnp.einsum("ikj,ij->ik", owners, similar, precision=lax.Precision.HIGHEST)
    scores = lax.psum(partial_value, "label") * temper
    likely = jax.nn.softmax(scores, axis=-1)
    target = jnp.where(jnp.arange(scores.shape[1]) < 2, 0.5, 0.0).astype(jnp.float32)
    pair_coef = ((likely - target[None, :]) * temper).astype(jnp.bfloat16)
    spread = jnp.einsum(
        "ik,ikj->ij", pair_coef.astype(jnp.float32), owners, precision=lax.Precision.HIGHEST
    ).astype(jnp.bfloat16)
    query_terms = jnp.dot(spread, label_bf, preferred_element_type=jnp.float32)
    query_grad = lax.psum(query_terms, "label")
    grad_part = jnp.einsum("ij,id->jd", spread, queries, preferred_element_type=jnp.float32)
    count_part = jnp.sum(owners, axis=(0, 1))
    label_grad, counts = lax.psum((grad_part, count_part), "query")
    out_grad = label_grad.astype(jnp.bfloat16)
    hidden_grad = jnp.dot(out_grad, down_weight, preferred_element_type=jnp.float32) / text_len
    token_grad = jnp.broadcast_to(
        hidden_grad[:, None, :], (label_rows, text_len, unit_cols)
    ).reshape(label_rows * text_len, unit_cols)
    preact_grad = jax.vjp(gelu_tanh, preact)[1](token_grad)[0].astype(jnp.bfloat16)
    joined = lax.psum_scatter(
        jnp.concatenate(
            (
                lax.dot_general(
                    text_rows,
                    preact_grad,
                    (((0,), (0,)), ((), ())),
                    preferred_element_type=jnp.float32,
                ),
                jnp.einsum(
                    "ld,lf->df",
                    out_grad.astype(jnp.float32),
                    pooled_hidden,
                    precision=lax.Precision.HIGHEST,
                ),
            ),
            axis=1,
        ),
        "label",
        scatter_dimension=0,
        tiled=True,
    )
    up_part = joined[:, :unit_cols]
    down_part = joined[:, unit_cols:]
    touched = (counts > 0.5)[:, None]
    moment_step = beta_one * moments + (1.0 - beta_one) * label_grad
    second_step = beta_two * seconds + (1.0 - beta_two) * label_grad * label_grad
    update = (
        learn_rate * (moment_step / first_fix) / (jnp.sqrt(second_step / second_fix) + adam_eps)
    )
    free_new = jnp.where(touched, free_vectors - update, free_vectors)
    moments_new = jnp.where(touched, moment_step, moments)
    seconds_new = jnp.where(touched, second_step, seconds)
    return (free_new, moments_new, seconds_new, query_grad, up_part, down_part)


def solution(mesh):
    placed = (
        P("query", None),
        P("query", None),
        P("label", None, None),
        P(None, "query"),
        P(None, "query"),
        P("label", None),
        P("label", None),
        P("label", None),
    )
    return jax.shard_map(
        body,
        mesh=mesh,
        in_specs=placed,
        out_specs=(
            P("label", None),
            P("label", None),
            P("label", None),
            P("query", None),
            P("label", "query"),
            P("label", "query"),
        ),
        check_vma=False,
    )
```

profile of v0, /device:TPU:25, one launch (start us, length us, event | category | flops | bytes accessed | tf_op | source)
XLA Modules:
  0.0 643.8 jit_solution(12416014666471665310)
XLA Ops:
  7.2 0.0 copy-start
  7.2 0.0 all-reduce.6.cloned.1.call-start
  7.2 1.0 copy-done
  8.2 0.0 copy-start.2
  8.2 6.1 convert_reduce_fusion.1
  14.4 0.0 copy-start.8
  14.4 0.0 copy-start.5
  14.4 0.0 copy-start.4
  14.4 0.0 copy-done.2
  14.4 1.3 fusion.16
  15.7 0.0 all-reduce.6.cloned.1.call-update
  15.7 0.0 all-reduce.8.cloned.1.call-start
  15.8 2.9 convert_reduce_fusion
  18.7 0.0 copy-done.8
  18.7 75.3 %all-reduce.6.cloned.1.call-done = f32[64,768]{1,0:T(8,128)} async-done(((f32[64,768]{1,0:T(8,128)}), f32[64,768]{1,0:T(8,128)}) %all-reduce.6.cloned.1.call-update) | async-done | bytes 196624 | tf_op jit(solution)/shard_map/psum | solution.py:32
  94.0 0.0 copy-done.5
  94.0 1.0 add_convert_fusion
  95.0 0.0 copy-done.4
  95.0 0.2 convolution_bitcast_fusion.1
  95.2 0.1 select_reduce_fusion.1
  95.3 235.5 %psum.37 = f32[192,10]{0,1:T(8,128)S(1)} all-reduce(f32[192,10]{0,1:T(8,128)S(1)} %select_reduce_fusion.1), channel_id=1, replica_groups=mesh['label'=64,'query'=8] {'label'}, use_global_device_ids=true, to_apply=%region_5.0 | all-reduce | flops 1920 | bytes 15360 | tf_op jit(solution)/shard_map/psum | solution.py:42
  330.9 0.1 fusion.27
  330.9 0.2 convert_reduce_fusion.2
  331.2 0.1 copy.31
  331.3 0.9 fusion.32
  332.2 0.0 all-reduce.8.cloned.1.call-update
  332.2 0.0 all-reduce.10.cloned.1.call-start
  332.3 1.0 fusion.31
  333.3 83.8 %all-reduce.8.cloned.1.call-done = f32[64,768]{1,0:T(8,128)} async-done(((f32[64,768]{1,0:T(8,128)}), f32[64,768]{1,0:T(8,128)}) %all-reduce.8.cloned.1.call-update) | async-done | bytes 196624 | tf_op jit(solution)/shard_map/psum | solution.py:53
  417.1 0.0 copy-start.1
  417.1 1.3 convolution_multiply_fusion
  418.4 3.6 fusion.6
  422.0 0.0 copy-done.1
  422.0 0.0 copy-start.3
  422.0 1.4 convolution_bitcast_fusion
  423.5 0.0 copy-done.3
  423.5 0.7 fusion.14
  424.2 0.0 copy-start.6
  424.2 0.0 copy-start.7
  424.2 1.5 pad_maximum_fusion
  425.7 0.0 all-reduce.10.cloned.1.call-update
  425.7 1.3 dynamic-slice
  427.7 12.6 %psum.35 = f32[64]{0:T(128)S(1)} all-reduce(f32[64]{0:T(128)S(1)} %get-tuple-element.24), channel_id=1, replica_groups=mesh['label'=64,'query'=8] {'query'}, use_global_device_ids=true, to_apply=%region_1.0 | all-reduce | flops 64 | bytes 512 | tf_op jit(solution)/shard_map/psum | solution.py:53
  440.3 0.0 copy-done.6
  440.3 0.0 copy-done.7
  440.3 1.0 fusion.13
  441.3 191.3 %all-reduce.10.cloned.1.call-done = (f32[192,768]{1,0:T(8,128)}, f32[768,768]{0,1:T(8,128)}) async-done(((f32[192,768]{1,0:T(8,128)}, f32[768,768]{0,1:T(8,128)}), (f32[192,768]{1,0:T(8,128)}, f32[768,768]{0,1:T(8,128)})) %all-reduce.10.cloned.1.call-update) | async-done | bytes 2949136 | tf_op jit(solution)/shard_map/psum | solution.py:50
  632.7 1.3 fusion.30
  633.9 0.7 copy.20
  634.7 0.7 copy.21
  635.4 1.9 copy.41
  (5 shorter events, 0.1 us)
Async XLA Ops:
  7.2 1.1 copy-start
  7.2 86.8 %all-reduce.6.cloned.1.call-start = ((), (), s32[]{:S(2)}) async-start(), calls=%async_computation | async-start | bytes 393216 | tf_op jit(solution)/shard_map/psum | solution.py:32
  8.2 6.1 copy-start.2
  14.4 4.3 copy-start.8
  14.4 79.7 %copy-start.5 = (f32[64,768]{1,0:T(8,128)S(1)}, f32[64,768]{1,0:T(8,128)}, u32[]{:S(2)}) copy-start(f32[64,768]{1,0:T(8,128)} %param.13) | copy-start | bytes 589828
  14.4 80.6 %copy-start.4 = (bf16[192,768]{1,0:T(8,128)(2,1)S(1)}, bf16[192,768]{1,0:T(8,128)(2,1)}, u32[]{:S(2)}) copy-start(bf16[192,768]{1,0:T(8,128)(2,1)} %param.8) | copy-start | bytes 884740
  15.7 401.4 %all-reduce.8.cloned.1.call-start = ((), (), s32[]{:S(2)}) async-start(), calls=%async_computation.1 | async-start | bytes 393216 | tf_op jit(solution)/shard_map/psum | solution.py:53
  332.2 300.4 %all-reduce.10.cloned.1.call-start = ((), (), s32[]{:S(2)}) async-start(), calls=%async_computation.2 | async-start | bytes 5898240 | tf_op jit(solution)/shard_map/psum | solution.py:50
  417.1 4.9 copy-start.1
  422.0 1.5 copy-start.3
  424.2 16.2 %copy-start.6 = (f32[64,768]{1,0:T(8,128)S(1)}, f32[64,768]{1,0:T(8,128)}, u32[]{:S(2)}) copy-start(f32[64,768]{1,0:T(8,128)} %param.15) | copy-start | bytes 589828
  424.2 16.2 %copy-start.7 = (f32[64,768]{1,0:T(8,128)S(1)}, f32[64,768]{1,0:T(8,128)}, u32[]{:S(2)}) copy-start(f32[64,768]{1,0:T(8,128)} %param.14) | copy-start | bytes 589828
Sparse Core Ops, SparseCore 0:
  15.8 78.1 all-reduce.5
  332.3 84.7 all-reduce.7
  425.9 206.7 all-reduce.9
where the time goes:
time: 644 us
  waiting for transfers between devices  351 us (55%)
  blocking collectives  248 us (39%)
  between operations  14.6 us (2%)
  matrix products  13 us (2%)
  other arithmetic  10.4 us (2%)
  local copies, waits for them, and re-layouts  7.07 us (1%)
    psum x1, blocking collectives, body(): scores = lax.psum(partial_value, 'label') * temper  235 us
    psum x1, waiting for transfers between devices, body(): query_grad = lax.psum(query_terms, 'label')  191 us
    psum x1, waiting for transfers between devices, body(): label_grad, counts = lax.psum((grad_part, count_part), 'query')  83.8 us
    psum x1, waiting for transfers between devices, body(): encoded = lax.psum(encoded_part, 'query')  75.3 us
  transfers between devices with their start and end apart: 3, of which 3 were waited for; matrix products, arithmetic and copies ran while one was open for 1% of the time, Pallas kernels for 0%

commit v1 on v0

--- a/solution.py
+++ b/solution.py
@@ -2,6 +2,7 @@
 import jax.numpy as jnp
 from jax import lax
 from jax.sharding import PartitionSpec as P
+from jax.lax import all_gather
 
 beta_one = 0.9
 beta_two = 0.999
@@ -39,7 +40,7 @@
     ).astype(jnp.float32)
     similar = jnp.einsum("id,jd->ij", queries, label_bf, preferred_element_type=jnp.float32)
     partial_value = jnp.einsum("ikj,ij->ik", owners, similar, precision=lax.Precision.HIGHEST)
-    scores = lax.psum(partial_value, "label") * temper
+    scores = jnp.sum(all_gather(partial_value, "label"), axis=0) * temper
     likely = jax.nn.softmax(scores, axis=-1)
     target = jnp.where(jnp.arange(scores.shape[1]) < 2, 0.5, 0.0).astype(jnp.float32)
     pair_coef = ((likely - target[None, :]) * temper).astype(jnp.bfloat16)

time: 644 us -> 449 us (0.70)
  blocking collectives: 248 us -> 67.9 us
  waiting for transfers between devices: 351 us -> 335 us
    psum x1 -> x0, blocking collectives: 235 us -> none  [body(): scores = lax.psum(partial_value, 'label') * temper]
    all_gather x0 -> x1, blocking collectives: none -> 55.3 us  [body(): scores = jnp.sum(all_gather(partial_value, 'label'), axis=0) * temper]
    psum x1, waiting for transfers between devices: 83.8 us -> 68.7 us  [body(): label_grad, counts = lax.psum((grad_part, count_part), 'query')]
where the time goes in v1:
time: 449 us; the launch traced here: 448 us
  waiting for transfers between devices  335 us (75%)
  blocking collectives  67.9 us (15%)
  between operations  14.6 us (3%)
  matrix products  13 us (3%)
  other arithmetic  10.5 us (2%)
  local copies, waits for them, and re-layouts  7.07 us (2%)
    psum x1, waiting for transfers between devices, body(): query_grad = lax.psum(query_terms, 'label')  191 us
    psum x1, waiting for transfers between devices, body(): encoded = lax.psum(encoded_part, 'query')  75.3 us
    psum x1, waiting for transfers between devices, body(): label_grad, counts = lax.psum((grad_part, count_part), 'query')  68.7 us
    all_gather x1, blocking collectives, body(): scores = jnp.sum(all_gather(partial_value, 'label'), axis=0) * temper  55.3 us
    psum x1, blocking collectives, body(): label_grad, counts = lax.psum((grad_part, count_part), 'query')  12.6 us
  transfers between devices with their start and end apart: 3, of which 3 were waited for; matrix products, arithmetic and copies ran while one was open for 1% of the time, Pallas kernels for 0%

profile of v1, /device:TPU:25, one launch (start us, length us, event | category | flops | bytes accessed | tf_op | source)
XLA Modules:
  0.0 448.2 jit_solution(595944350902048428)
XLA Ops:
  7.2 0.0 copy-start
  7.2 0.0 all-reduce.6.cloned.1.call-start
  7.2 1.0 copy-done
  8.2 0.0 copy-start.2
  8.2 6.1 %convert_reduce_fusion.1 = (f32[64,384]{1,0:T(8,128)S(1)}, f32[2048,384]{1,0:T(8,128)}) fusion(bf16[2048,768]{1,0:T(8,128)(2,1)} %bitcast.41, bf16[768,384]{1,0:T(8,128)(2,1)S(1)} %copy-done), kind=kOutput, calls=%fused_computation.15 | convolution fusion | flops 1216585728 | bytes 6979584 | tf_op jit(solution)/shard_map/dot_general | solution.py:24
  14.4 0.0 copy-start.8
  14.4 0.0 copy-start.5
  14.4 0.0 copy-start.4
  14.4 0.0 copy-done.2
  14.4 1.3 fusion.16
  15.7 0.0 all-reduce.6.cloned.1.call-update
  15.7 0.0 all-reduce.8.cloned.1.call-start
  15.8 2.9 convert_reduce_fusion
  18.7 0.0 copy-done.8
  18.7 75.3 %all-reduce.6.cloned.1.call-done = f32[64,768]{1,0:T(8,128)} async-done(((f32[64,768]{1,0:T(8,128)}), f32[64,768]{1,0:T(8,128)}) %all-reduce.6.cloned.1.call-update) | async-done | bytes 196624 | tf_op jit(solution)/shard_map/psum | solution.py:33
  94.0 0.0 copy-done.5
  94.0 1.0 add_convert_fusion
  95.0 0.0 copy-done.4
  95.0 0.2 convolution_bitcast_fusion.1
  95.2 0.1 select_reduce_fusion.1
  95.3 55.3 %all-gather.1 = f32[64,192,10]{1,2,0:T(8,128)S(1)} all-gather(f32[1,192,10]{1,2,0:T(8,128)S(1)} %bitcast.43), channel_id=2, replica_groups=mesh['label'=64,'query'=8] {'label'}, dimensions={0}, use_global_device_ids=true | all-gather | bytes 499200 | tf_op jit(solution)/shard_map/all_gather | solution.py:43
  150.6 0.1 reduce_sum.48
  150.8 0.1 fusion.27
  150.8 0.2 convert_reduce_fusion.2
  151.1 0.1 copy.34
  151.2 0.9 fusion.32
  152.1 0.0 all-reduce.8.cloned.1.call-update
  152.1 0.0 all-reduce.10.cloned.1.call-start
  152.1 1.0 fusion.31
  153.2 68.7 %all-reduce.8.cloned.1.call-done = f32[64,768]{1,0:T(8,128)} async-done(((f32[64,768]{1,0:T(8,128)}), f32[64,768]{1,0:T(8,128)}) %all-reduce.8.cloned.1.call-update) | async-done | bytes 196624 | tf_op jit(solution)/shard_map/psum | solution.py:54
  221.8 0.0 copy-start.1
  221.8 1.3 convolution_multiply_fusion
  223.1 3.6 fusion.6
  226.7 0.0 copy-done.1
  226.7 0.0 copy-start.3
  226.7 1.4 convolution_bitcast_fusion
  228.2 0.0 copy-done.3
  228.2 0.7 fusion.14
  228.9 0.0 copy-start.6
  228.9 0.0 copy-start.7
  228.9 1.5 pad_maximum_fusion
  230.4 0.0 all-reduce.10.cloned.1.call-update
  230.5 1.3 dynamic-slice
  232.4 12.6 %psum.28 = f32[64]{0:T(128)S(1)} all-reduce(f32[64]{0:T(128)S(1)} %get-tuple-element.30), channel_id=1, replica_groups=mesh['label'=64,'query'=8] {'query'}, use_global_device_ids=true, to_apply=%region_1.0 | all-reduce | flops 64 | bytes 512 | tf_op jit(solution)/shard_map/psum | solution.py:54
  245.0 0.0 copy-done.6
  245.0 0.0 copy-done.7
  245.0 1.0 fusion.13
  246.0 191.0 %all-reduce.10.cloned.1.call-done = (f32[192,768]{1,0:T(8,128)}, f32[768,768]{0,1:T(8,128)}) async-done(((f32[192,768]{1,0:T(8,128)}, f32[768,768]{0,1:T(8,128)}), (f32[192,768]{1,0:T(8,128)}, f32[768,768]{0,1:T(8,128)})) %all-reduce.10.cloned.1.call-update) | async-done | bytes 2949136 | tf_op jit(solution)/shard_map/psum | solution.py:51
  437.0 1.3 fusion.30
  438.3 0.7 copy.23
  439.0 0.7 copy.24
  439.7 1.9 copy.44
  (5 shorter events, 0.1 us)
Async XLA Ops:
  7.2 1.1 copy-start
  7.2 86.8 %all-reduce.6.cloned.1.call-start = ((), (), s32[]{:S(2)}) async-start(), calls=%async_computation | async-start | bytes 393216 | tf_op jit(solution)/shard_map/psum | solution.py:33
  8.2 6.1 %copy-start.2 = (bf16[768,384]{1,0:T(8,128)(2,1)S(1)}, bf16[768,384]{1,0:T(8,128)(2,1)}, u32[]{:S(2)}) copy-start(bf16[768,384]{1,0:T(8,128)(2,1)} %param.12) | copy-start | bytes 1769476
  14.4 4.3 copy-start.8
  14.4 79.7 %copy-start.5 = (f32[64,768]{1,0:T(8,128)S(1)}, f32[64,768]{1,0:T(8,128)}, u32[]{:S(2)}) copy-start(f32[64,768]{1,0:T(8,128)} %param.13) | copy-start | bytes 589828
  14.4 80.6 %copy-start.4 = (bf16[192,768]{1,0:T(8,128)(2,1)S(1)}, bf16[192,768]{1,0:T(8,128)(2,1)}, u32[]{:S(2)}) copy-start(bf16[192,768]{1,0:T(8,128)(2,1)} %param.8) | copy-start | bytes 884740
  15.7 206.1 %all-reduce.8.cloned.1.call-start = ((), (), s32[]{:S(2)}) async-start(), calls=%async_computation.1 | async-start | bytes 393216 | tf_op jit(solution)/shard_map/psum | solution.py:54
  152.1 284.9 %all-reduce.10.cloned.1.call-start = ((), (), s32[]{:S(2)}) async-start(), calls=%async_computation.2 | async-start | bytes 5898240 | tf_op jit(solution)/shard_map/psum | solution.py:51
  221.8 4.9 %copy-start.1 = (bf16[64,32,768]{2,1,0:T(8,128)(2,1)S(1)}, bf16[64,32,768]{2,1,0:T(8,128)(2,1)}, u32[]{:S(2)}) copy-start(bf16[64,32,768]{2,1,0:T(8,128)(2,1)} %param.10) | copy-start | bytes 9437188
  226.7 1.5 copy-start.3
  228.9 16.2 %copy-start.6 = (f32[64,768]{1,0:T(8,128)S(1)}, f32[64,768]{1,0:T(8,128)}, u32[]{:S(2)}) copy-start(f32[64,768]{1,0:T(8,128)} %param.15) | copy-start | bytes 589828
  228.9 16.2 %copy-start.7 = (f32[64,768]{1,0:T(8,128)S(1)}, f32[64,768]{1,0:T(8,128)}, u32[]{:S(2)}) copy-start(f32[64,768]{1,0:T(8,128)} %param.14) | copy-start | bytes 589828
Sparse Core Ops, SparseCore 0:
  15.8 78.1 all-reduce.5
  152.2 69.5 all-reduce.7
  230.6 206.4 all-reduce.9
